TPU v7x, 768 devices: a whole 4x8x12 slice. The times are simulated.
768 devices in a mesh: blk: 24 (over z, x_hi), rep: 32 (over x_lo, y, core).
Axes of the slice: x: 4 (x_hi: 2, x_lo: 2; x = x_hi * 2 + x_lo), y: 8, z: 12, core: 2. Of those that a mesh axis runs over, the one named last changes fastest.
Arguments:
- feats: bfloat16 [32, 6144, 128], P('rep', 'blk'), may hold values from -6 to 6
- cotan: bfloat16 [32, 6144, 256], P('rep', 'blk'), may hold values from -6 to 6
- weight: bfloat16 [128, 256], replicated, may hold values from -0.5 to 0.5
- cycle_adj: bfloat16 [32, 6144, 6144], P('rep', 'blk'), as said below
- remote_adj: bfloat16 [32, 6144, 1024], P('rep', 'blk'), may hold values from -0.25 to 0.25
- send_ids: int32 [32, 24, 32, 32], P('rep', 'blk'), may hold values from 0 to 255
- send_count: int32 [32, 24, 32], P('rep', 'blk'), may hold values from 1 to 32, as said below
Outputs:
- output_rows: bfloat16 [32, 6144, 256], P('rep', 'blk')
- grad_feats: float32 [32, 6144, 128], P('rep', 'blk')
- grad_weight: float32 [128, 256], replicated
Inputs may be any that keep to these rules, and one draw needn't show every extreme that they name: cycle_adj[r] is symmetric: entry (i, j) equals entry (j, i) exactly. `send_count`: every row block has 32 live slots toward at least one group.
All inputs are finite; a program needn't handle non-finite values.
Results may differ from a plain program's by a relative error of at most 0.017.
Values may be sent and summed in bfloat16 or wider, within the bound.
A program may use at most 32 MiB of HBM per device.

v0:
```python
import math

import jax
import jax.numpy as jnp
from jax import lax
from jax.sharding import PartitionSpec as P


def gelu_tanh(values):
    return jax.nn.gelu(values, approximate=True)


def local(feats, cotan, weight, cycle_adj, remote_adj, send_ids, send_count):
    local_x = feats[0]
    adjacency = cycle_adj[0]
    far_adj = remote_adj[0]
    row_ids = send_ids[0, 0]
    live_counts = send_count[0, 0]
    row_count = local_x.shape[0]
    feat_width = local_x.shape[1]
    groups = row_ids.shape[0]
    slot_count = row_ids.shape[1]
    zero_rows = jnp.zeros((row_count, feat_width), jnp.float32)
    columns = adjacency
    cycle_agg = jnp.dot(
        columns,
        lax.all_gather(local_x, "blk", axis=0, tiled=True),
        preferred_element_type=jnp.float32,
    )
    live_slots = lax.broadcasted_iota(jnp.int32, (groups, slot_count), 1) < live_counts[:, None]
    picked = jnp.take(local_x, row_ids.reshape(-1), axis=0).reshape(groups, slot_count, feat_width)
    outgoing = jnp.where(live_slots[:, :, None], picked, jnp.zeros_like(picked))
    arrived = lax.all_to_all(outgoing, "rep", split_axis=0, concat_axis=0, tiled=True)
    far_agg = jnp.dot(
        far_adj,
        arrived.reshape(groups * slot_count, feat_width),
        preferred_element_type=jnp.float32,
    )
    agg = (cycle_agg + far_agg).astype(jnp.bfloat16)
    pre_act = jnp.dot(agg, weight, preferred_element_type=jnp.float32)
    activated, back_fn = jax.vjp(gelu_tanh, pre_act)
    output_rows = activated.astype(jnp.bfloat16)
    dpre = back_fn(cotan[0].astype(jnp.float32))[0].astype(jnp.bfloat16)
    node_total = row_count * lax.axis_size("blk") * lax.axis_size("rep")
    partial_grad = lax.dot_general(
        agg, dpre, (((0,), (0,)), ((), ())), preferred_element_type=jnp.float32
    )
    grad_weight = lax.psum(partial_grad, ("blk", "rep")) * (1.0 / math.sqrt(node_total))
    proj = lax.dot_general(
        dpre, weight, (((1,), (1,)), ((), ())), preferred_element_type=jnp.float32
    ).astype(jnp.bfloat16)
    columns = adjacency
    cycle_back = lax.psum_scatter(
        lax.dot_general(
            columns, proj, (((0,), (0,)), ((), ())), preferred_element_type=jnp.float32
        ).astype(jnp.bfloat16),
        "blk",
        scatter_dimension=0,
        tiled=True,
    ).astype(jnp.float32)
    far_terms = lax.dot_general(
        far_adj, proj, (((0,), (0,)), ((), ())), preferred_element_type=jnp.float32
    )
    far_terms = far_terms.astype(jnp.bfloat16).reshape(groups, slot_count, feat_width)
    returned = lax.all_to_all(far_terms, "rep", split_axis=0, concat_axis=0, tiled=True)
    masked = jnp.where(
        live_slots[:, :, None],
        returned.astype(jnp.float32),
        jnp.zeros((groups, slot_count, feat_width), jnp.float32),
    )
    far_back = zero_rows.at[row_ids.reshape(-1)].add(
        masked.reshape(groups * slot_count, feat_width)
    )
    grad_feats = cycle_back + far_back
    return (output_rows[None], grad_feats[None], grad_weight)


def solution(mesh):
    return jax.shard_map(
        local,
        mesh=mesh,
        in_specs=(
            P("rep", "blk", None),
            P("rep", "blk", None),
            P(),
            P("rep", "blk", None),
            P("rep", "blk", None),
            P("rep", "blk", None, None),
            P("rep", "blk", None),
        ),
        out_specs=(P("rep", "blk", None), P("rep", "blk", None), P()),
        check_vma=False,
    )
```

profile of v0, /device:TPU:1, one launch (start us, length us, event | category | flops | bytes accessed | tf_op | source)
XLA Modules:
  0.0 993.9 jit_solution(16053519720161103812)
XLA Ops:
  7.2 0.0 copy-start
  7.2 0.0 all-gather.3.cloned.1.call-start
  7.2 0.7 all-gather.3.cloned.1.call-update
  7.9 0.0 all-reduce.2.cloned.1.call-start
  8.0 1.0 reshape_squeeze.7
  8.9 3.7 gather_fusion
  12.7 0.8 iota_compare_fusion
  13.5 0.3 select_select_fusion
  13.8 0.0 copy-start.2
  13.8 25.3 %all_to_all.10 = bf16[32,32,128]{2,1,0:T(8,128)(2,1)S(1)} all-to-all(bf16[32,32,128]{2,1,0:T(8,128)(2,1)S(1)} %select_select_fusion), channel_id=1, replica_groups=mesh['blk'=24,'rep'=32] {'rep'}, dimensions={0} | all-to-all | bytes 524288 | tf_op jit(solution)/shard_map/all_to_all | solution.py:33
  39.2 1.3 convolution_bitcast_fusion
  40.5 94.1 %all-gather.3.cloned.1.call-done = bf16[1,6144,128]{2,1,0:T(8,128)(2,1)} async-done(((bf16[1,256,128]{2,1,0:T(8,128)(2,1)}), bf16[1,6144,128]{2,1,0:T(8,128)(2,1)}) %all-gather.3.cloned.1.call-update) | async-done | bytes 1572880 | tf_op jit(solution)/shard_map/all_gather | solution.py:27
  134.6 0.0 copy-done
  134.6 2.4 fusion.11
  137.0 0.0 copy-done.2
  137.0 1.9 fusion.20
  138.9 0.2 convolution_convert_fusion.2
  139.1 0.9 fusion.29
  140.0 0.0 all-reduce.2.cloned.1.call-update
  140.0 0.0 reduce-scatter.2.cloned.1.call-start
  140.0 1.8 fusion
  141.8 0.0 reduce-scatter.2.cloned.1.call-update
  141.8 1.3 fusion.5
  143.1 0.8 copy.15
  143.9 13.9 %all-to-all-start.1 = ((bf16[32,32,128]{2,1,0:T(8,128)(2,1)}), bf16[32,32,128]{2,1,0:T(8,128)(2,1)S(1)}, u32[]{:S(2)}, u32[]{:S(2)}) async-start(bf16[32,32,128]{2,1,0:T(8,128)(2,1)} %bitcast.60), calls=%async_computation.2 | async-start | bytes 524288 | tf_op jit(solution)/shard_map/all_to_all | solution.py:65
  157.9 441.4 %all-reduce.2.cloned.1.call-done = f32[128,256]{1,0:T(8,128)} async-done(((f32[128,256]{1,0:T(8,128)}), f32[128,256]{1,0:T(8,128)}) %all-reduce.2.cloned.1.call-update) | async-done | bytes 131088 | tf_op jit(solution)/shard_map/psum | solution.py:48
  599.3 1.6 broadcast_multiply_fusion
  600.8 0.0 all-to-all-done.1
  600.8 1.0 convert_select_fusion
  601.8 377.4 %reduce-scatter.2.cloned.1.call-done = bf16[256,128]{0,1:T(8,128)(2,1)} async-done(((bf16[6144,128]{0,1:T(8,128)(2,1)}), bf16[256,128]{0,1:T(8,128)(2,1)}) %reduce-scatter.2.cloned.1.call-update) | async-done | bytes 65552 | tf_op jit(solution)/shard_map/reduce_scatter | solution.py:53
  979.2 0.9 copy.16
  980.2 6.5 scatter_fusion
  986.7 0.0 copy-start.1
  986.7 0.6 copy-done.1
  (2 shorter events, 0.0 us)
Async XLA Ops:
  7.2 127.4 %copy-start = (bf16[1,256,6144]{2,1,0:T(8,128)(2,1)S(1)}, bf16[1,256,6144]{2,1,0:T(8,128)(2,1)}, u32[]{:S(2)}) copy-start(bf16[1,256,6144]{2,1,0:T(8,128)(2,1)} %param.10) | copy-start | bytes 9437188
  7.2 127.4 %all-gather.3.cloned.1.call-start = ((), (), s32[]{:S(2)}) async-start(), calls=%async_computation.5 | async-start | bytes 1638400 | tf_op jit(solution)/shard_map/all_gather | solution.py:27
  7.9 591.4 %all-reduce.2.cloned.1.call-start = ((), (), s32[]{:S(2)}) async-start(), calls=%async_computation.4 | async-start | bytes 262144 | tf_op jit(solution)/shard_map/psum | solution.py:48
  13.8 123.2 %copy-start.2 = (bf16[128,256]{1,0:T(8,128)(2,1)S(1)}, bf16[128,256]{1,0:T(8,128)(2,1)}, u32[]{:S(2)}) copy-start(bf16[128,256]{1,0:T(8,128)(2,1)} %param.9) | copy-start | bytes 196612
  140.0 839.3 %reduce-scatter.2.cloned.1.call-start = ((), (), s32[]{:S(2)}) async-start(), calls=%async_computation.3 | async-start | bytes 1638400 | tf_op jit(solution)/shard_map/reduce_scatter | solution.py:53
  143.9 456.9 %all-to-all-start.1 = ((bf16[32,32,128]{2,1,0:T(8,128)(2,1)}), bf16[32,32,128]{2,1,0:T(8,128)(2,1)S(1)}, u32[]{:S(2)}, u32[]{:S(2)}) async-start(bf16[32,32,128]{2,1,0:T(8,128)(2,1)} %bitcast.60), calls=%async_computation.2 | async-start | bytes 524288 | tf_op jit(solution)/shard_map/all_to_all | solution.py:65
  986.7 0.7 copy-start.1
Sparse Core Ops, SparseCore 0:
  11.6 122.9 all-gather.2
  140.6 458.6 all-reduce.1
  605.0 374.1 reduce-scatter.1
where the time goes:
time: 1000 us; the launch traced here: 994 us
  waiting for transfers between devices  914 us (91%)
  blocking collectives  25.3 us (3%)
  starting transfers between devices  14 us (1%)
  between operations  13.9 us (1%)
  other arithmetic  10.2 us (1%)
    psum x1, waiting for transfers between devices, local(): lax.psum(partial_grad, ('blk', 'rep')) * (1.0 / math.sqrt(node_total))  441 us
    reduce_scatter x1, waiting for transfers between devices, local(): lax.psum_scatter(lax.dot_general(columns, proj, (((0,), (0,)), ((), ())),...  377 us
    all_gather x1, waiting for transfers between devices, local(): lax.all_gather(local_x, 'blk', axis=0, tiled=True)  94.1 us
    all_to_all x1, blocking collectives, local(): lax.all_to_all(outgoing, 'rep', split_axis=0, concat_axis=0, tiled=True)  25.3 us
  transfers between devices with their start and end apart: 4, of which 3 were waited for; matrix products, arithmetic and copies ran while one was open for 1% of the time, Pallas kernels for 0%

commit v1 on v0

v1 whole, which is shorter than its diff:
```python
import functools
import math

import jax
import jax.numpy as jnp
from jax import lax
from jax.experimental import pallas as pl
from jax.experimental.pallas import tpu as pltpu
from jax.sharding import PartitionSpec as P

MESH = pl.DeviceIdType.MESH
F32 = jnp.float32
BF16 = jnp.bfloat16


def dot(a, b, dims=((1,), (0,))):
    return lax.dot_general(a, b, (dims, ((), ())), preferred_element_type=F32)


def layer_kernel(
    n_blk, n_rep,
    feats, cotan, weight, adj_hbm, far_hbm, ids, counts,
    out_rows, grad_feats, grad_weight,
    adj, far, near_x, near_p, total, pick, sent, arrived, back, returned, part, sum_rep, sum_blk, whole,
    load_sem, ring_send, ring_recv, pair_recv, swap_send, swap_recv, grad_send, grad_recv,
):
    blk = lax.axis_index("blk")
    rep = lax.axis_index("rep")
    rows, width = feats.shape[1], feats.shape[2]
    groups, slots = ids.shape[2], ids.shape[3]
    slot_total = groups * slots
    n_z = n_blk // 2
    reach = n_z // 2
    z = blk // 2
    x_hi = lax.rem(blk, 2)
    half = rows // 2
    piece = part.shape[1]

    barrier = pltpu.get_barrier_semaphore()

    def greet_rep(i, carry):
        pl.semaphore_signal(barrier, inc=1, device_id={"rep": lax.rem(rep + i, n_rep)}, device_id_type=MESH)
        return carry

    def greet_blk(i, carry):
        pl.semaphore_signal(barrier, inc=1, device_id={"blk": lax.rem(blk + i, n_blk)}, device_id_type=MESH)
        return carry

    lax.fori_loop(1, n_rep, greet_rep, 0)
    lax.fori_loop(1, n_blk, greet_blk, 0)

    load_adj = pltpu.make_async_copy(adj_hbm.at[0], adj, load_sem.at[0])
    load_far = pltpu.make_async_copy(far_hbm.at[0], far, load_sem.at[1])
    load_adj.start()
    load_far.start()

    def line(z_at, other):
        return lax.rem(z_at + n_z, n_z) * 2 + (1 - x_hi if other else x_hi)

    ups = (line(z + 1, 0), line(z - 1, 0))

    def hop(near, phase, way, other, d, idx):
        if isinstance(d, int) and d == reach:
            span = pl.ds(way * half, half)
        else:
            span = pl.ds(0, rows)
        return pltpu.make_async_remote_copy(
            src_ref=near.at[idx, span], dst_ref=near.at[idx, span],
            send_sem=ring_send.at[phase], recv_sem=ring_recv.at[phase, way, other, d - 1],
            device_id={"blk": ups[way]}, device_id_type=MESH,
        )

    def pair(near, phase, idx):
        return pltpu.make_async_remote_copy(
            src_ref=near.at[idx], dst_ref=near.at[idx],
            send_sem=ring_send.at[phase], recv_sem=pair_recv.at[phase],
            device_id={"blk": line(z, 1)}, device_id_type=MESH,
        )

    def add_block(near, idx):
        columns = pl.ds(pl.multiple_of(idx * rows, rows), rows)
        total[...] += dot(adj[:, columns], near[idx])

    def came(way, other, d):
        return line(z - d if way == 0 else z + d, other)

    def ring_open(near, phase):
        hop(near, phase, 0, 0, 1, blk).start()
        hop(near, phase, 1, 0, 1, blk).start()
        pair(near, phase, blk).start()

    def ring_pair(near, phase):
        idx = line(z, 1)
        pair(near, phase, idx).wait_recv()
        hop(near, phase, 0, 1, 1, idx).start()
        hop(near, phase, 1, 1, 1, idx).start()
        add_block(near, idx)

    def ring_step(near, phase, d, last):
        for other in (0, 1):
            for way in (0, 1):
                idx = came(way, other, d)
                hop(near, phase, way, other, d, idx).wait_recv()
                hop(near, phase, way, other, reach if last else d + 1, idx).start()
            for way in (0, 1):
                add_block(near, came(way, other, d))

    def ring_steps(near, phase, first, stop):
        def step(d, carry):
            ring_step(near, phase, d, False)
            return carry
        lax.fori_loop(first, stop, step, 0)

    def ring_close(near, phase):
        for other in (0, 1):
            idx = came(0, other, reach)
            for way in (0, 1):
                hop(near, phase, way, other, reach, idx).wait_recv()
            add_block(near, idx)

    def ring_drain(near, phase):
        whole_ring = near.at[pl.ds(0, n_blk - 1)]
        pltpu.make_async_copy(whole_ring, whole_ring, ring_send.at[phase]).wait()

    def to_reps(src, dst, send_sem, recv_sem):
        def send(i, carry):
            peer = lax.rem(rep + i, n_rep)
            pltpu.make_async_remote_copy(
                src_ref=src(peer), dst_ref=dst, send_sem=send_sem, recv_sem=recv_sem,
                device_id={"rep": peer}, device_id_type=MESH,
            ).start()
            return carry
        lax.fori_loop(1, n_rep, send, 0)

    def wait_all(ref, count, sem):
        span = ref.at[pl.ds(0, count)]
        pltpu.make_async_copy(span, span, sem).wait()

    spread = lax.broadcasted_iota(jnp.int32, (slots, slot_total), 1)
    within = spread - (spread // slots) * slots
    place = lax.broadcasted_iota(jnp.int32, (slots, slot_total), 0)
    per_slot = jnp.where(within == place, 1.0, 0.0).astype(BF16)
    spread_g = lax.broadcasted_iota(jnp.int32, (groups, slot_total), 1)
    own_group = (spread_g // slots) == lax.broadcasted_iota(jnp.int32, (groups, slot_total), 0)
    per_group = jnp.where(own_group, 1.0, 0.0).astype(BF16)
    ids_wide = dot(ids[0, 0].astype(F32).astype(BF16), per_slot)
    ids_row = jnp.sum(jnp.where(own_group, ids_wide, 0.0), axis=0, keepdims=True)
    counts_low = jnp.broadcast_to(counts[0].astype(F32), (8, groups)).astype(BF16)
    counts_row = dot(counts_low, per_group)[0:1]
    live = within[0:1].astype(F32) < counts_row
    ids_row = jnp.where(live, ids_row, -1.0).astype(jnp.int32)
    row_iota = lax.broadcasted_iota(jnp.int32, (rows, slot_total), 0)
    pick[...] = jnp.where(row_iota == ids_row, 1.0, 0.0).astype(BF16)
    own_feats = feats[0]
    near_x[blk] = own_feats
    sent[...] = dot(pick[...], own_feats, ((0,), (0,))).astype(BF16).reshape(groups, slots, width)

    pl.semaphore_wait(barrier, n_rep - 1 + n_blk - 1)

    ring_open(near_x, 0)
    to_reps(lambda peer: sent.at[peer], arrived.at[rep], swap_send.at[0], swap_recv.at[0])
    arrived[rep] = sent[rep]
    total[...] = jnp.zeros_like(total)
    load_adj.wait()
    add_block(near_x, blk)
    ring_pair(near_x, 0)
    ring_steps(near_x, 0, 1, reach - 1)
    ring_step(near_x, 0, reach - 1, True)
    load_far.wait()
    wait_all(arrived, n_rep - 1, swap_recv.at[0])
    total[...] += dot(far[...], arrived[...].reshape(slot_total, width))
    ring_close(near_x, 0)

    agg = total[...].astype(BF16)
    pre = dot(agg, weight[...])
    scale, cubic = 0.7978845608028654, 0.044715
    square = pre * pre
    bend = jnp.tanh(scale * pre * (1.0 + cubic * square))
    slope = 0.5 * (1.0 + bend) + 0.5 * pre * (1.0 - bend * bend) * (scale * (1.0 + 3.0 * cubic * square))
    dpre = (cotan[0].astype(F32) * slope).astype(BF16)
    proj = dot(dpre, weight[...], ((1,), (1,))).astype(BF16)
    near_p[blk] = proj
    ring_open(near_p, 1)
    share = dot(agg, dpre, ((0,), (0,)))
    per_half = n_rep // 2
    part[pl.ds(0, per_half)] = share[:, :width].reshape(per_half, piece, width)
    part[pl.ds(per_half, per_half)] = share[:, width:].reshape(per_half, piece, width)
    to_reps(lambda peer: part.at[peer], sum_rep.at[rep], grad_send.at[0], grad_recv.at[0])
    sum_rep[rep] = part[rep]
    back[...] = dot(far[...], proj, ((0,), (0,))).astype(BF16).reshape(groups, slots, width)
    to_reps(lambda peer: back.at[peer], returned.at[rep], swap_send.at[1], swap_recv.at[1])
    returned[rep] = back[rep]
    out_rows[0] = (0.5 * pre * (1.0 + bend)).astype(BF16)

    total[...] = jnp.zeros_like(total)
    add_block(near_p, blk)
    ring_pair(near_p, 1)
    first = min(3, reach - 1)
    ring_steps(near_p, 1, 1, first)

    wait_all(sum_rep, n_rep - 1, grad_recv.at[0])
    sum_blk[blk] = jnp.sum(sum_rep[...], axis=0)

    def send_blk(i, carry):
        pltpu.make_async_remote_copy(
            src_ref=sum_blk.at[blk], dst_ref=sum_blk.at[blk], send_sem=grad_send.at[1], recv_sem=grad_recv.at[1],
            device_id={"blk": lax.rem(blk + i, n_blk)}, device_id_type=MESH,
        ).start()
        return carry
    lax.fori_loop(1, n_blk, send_blk, 0)

    ring_steps(near_p, 1, first, reach - 1)
    wait_all(sum_blk, n_blk - 1, grad_recv.at[1])
    nodes = rows * n_blk * n_rep
    whole[rep] = jnp.sum(sum_blk[...], axis=0) * (1.0 / math.sqrt(nodes))
    to_reps(lambda peer: whole.at[rep], whole.at[rep], grad_send.at[2], grad_recv.at[2])
    ring_step(near_p, 1, reach - 1, True)
    wait_all(returned, n_rep - 1, swap_recv.at[1])
    total[...] += dot(pick[...], returned[...].reshape(slot_total, width))
    ring_close(near_p, 1)
    grad_feats[0] = total[...]
    wait_all(whole, n_rep - 1, grad_recv.at[2])
    flat = per_half * piece
    grad_weight[:, :width] = whole[pl.ds(0, per_half)].reshape(flat, width)
    grad_weight[:, width:] = whole[pl.ds(per_half, per_half)].reshape(flat, width)

    ring_drain(near_x, 0)
    ring_drain(near_p, 1)
    wait_all(sent, n_rep - 1, swap_send.at[0])
    wait_all(back, n_rep - 1, swap_send.at[1])
    wait_all(part, n_rep - 1, grad_send.at[0])
    wait_all(sum_blk, n_blk - 1, grad_send.at[1])
    wait_all(whole, n_rep - 1, grad_send.at[2])


def local(n_blk, n_rep, feats, cotan, weight, cycle_adj, remote_adj, send_ids, send_count):
    rows, width = feats.shape[1:]
    hidden = cotan.shape[2]
    groups, slots = send_ids.shape[2:]
    total = n_blk * rows
    reach = n_blk // 4
    piece = hidden // n_rep * (width // 128)
    vmem = pl.BlockSpec(memory_space=pltpu.VMEM)
    anywhere = pl.BlockSpec(memory_space=pl.ANY)
    dma = pltpu.SemaphoreType.DMA
    return pl.pallas_call(
        functools.partial(layer_kernel, n_blk, n_rep),
        out_shape=(
            jax.ShapeDtypeStruct((1, rows, hidden), BF16),
            jax.ShapeDtypeStruct((1, rows, width), F32),
            jax.ShapeDtypeStruct((width, hidden), F32),
        ),
        in_specs=[vmem, vmem, vmem, anywhere, anywhere, vmem, vmem],
        out_specs=(vmem, vmem, vmem),
        scratch_shapes=[
            pltpu.VMEM((rows, total), BF16),
            pltpu.VMEM((rows, groups * slots), BF16),
            pltpu.VMEM((n_blk, rows, width), BF16),
            pltpu.VMEM((n_blk, rows, width), BF16),
            pltpu.VMEM((rows, width), F32),
            pltpu.VMEM((rows, groups * slots), BF16),
            pltpu.VMEM((groups, slots, width), BF16),
            pltpu.VMEM((groups, slots, width), BF16),
            pltpu.VMEM((groups, slots, width), BF16),
            pltpu.VMEM((groups, slots, width), BF16),
            pltpu.VMEM((n_rep, piece, width), F32),
            pltpu.VMEM((n_rep, piece, width), F32),
            pltpu.VMEM((n_blk, piece, width), F32),
            pltpu.VMEM((n_rep, piece, width), F32),
            dma((2,)),
            dma((2,)),
            dma((2, 2, 2, reach)),
            dma((2,)),
            dma((2,)),
            dma((2,)),
            dma((3,)),
            dma((3,)),
        ],
        compiler_params=pltpu.CompilerParams(
            collective_id=0, has_side_effects=True, vmem_limit_bytes=40 * 1024 * 1024
        ),
    )(feats, cotan, weight, cycle_adj, remote_adj, send_ids, send_count)


def solution(mesh):
    n_blk, n_rep = mesh.shape["blk"], mesh.shape["rep"]
    return jax.shard_map(
        functools.partial(local, n_blk, n_rep),
        mesh=mesh,
        in_specs=(
            P("rep", "blk", None),
            P("rep", "blk", None),
            P(),
            P("rep", "blk", None),
            P("rep", "blk", None),
            P("rep", "blk", None, None),
            P("rep", "blk", None),
        ),
        out_specs=(P("rep", "blk", None), P("rep", "blk", None), P()),
        check_vma=False,
    )
```

time: 1000 us -> 88.3 us (0.09)
  waiting for transfers between devices: 914 us -> 0 us
  Pallas kernels: 0 us -> 78.4 us
  blocking collectives: 25.3 us -> 0 us
  starting transfers between devices: 14 us -> 0 us
  between operations: 13.9 us -> 0.66 us
  other arithmetic: 10.2 us -> 0 us
    psum x1 -> x0, waiting for transfers between devices: 441 us -> none  [local(): lax.psum(partial_grad, ('blk', 'rep')) * (1.0 / math.sqrt(node_total))]
    reduce_scatter x1 -> x0, waiting for transfers between devices: 377 us -> none  [local(): lax.psum_scatter(lax.dot_general(columns, proj, (((0,), (0,)), ((), ())),...]
    all_gather x1 -> x0, waiting for transfers between devices: 94.1 us -> none  [local(): lax.all_gather(local_x, 'blk', axis=0, tiled=True)]
    pallas_call x0 -> x1, Pallas kernels: none -> 78.4 us  [local(): pl.pallas_call(functools.partial(layer_kernel, n_blk, n_rep), out_shape=(...]
    all_to_all x1 -> x0, blocking collectives: 25.3 us -> none  [local(): lax.all_to_all(outgoing, 'rep', split_axis=0, concat_axis=0, tiled=True)]
    all_to_all x1 -> x0, starting transfers between devices: 13.9 us -> none  [local(): lax.all_to_all(far_terms, 'rep', split_axis=0, concat_axis=0, tiled=True)]
  transfers between devices with their start and end apart: 4 -> 0, of which waited for: 3 -> 0; matrix products, arithmetic and copies ran while one was open for 1% -> 0% of each run, Pallas kernels for 0% -> 0%
where the time goes in v1:
time: 88.3 us; the launch traced here: 87.9 us
  Pallas kernels  78.4 us (89%)
  local copies, waits for them, and re-layouts  8.84 us (10%)
    pallas_call x1, Pallas kernels, local(): pl.pallas_call(functools.partial(layer_kernel, n_blk, n_rep), out_shape=(...  78.4 us
    unnamed x17, local copies, waits for them, and re-layouts  8.84 us

profile of v1, /device:TPU:1, one launch (start us, length us, event | category | flops | bytes accessed | tf_op | source)
XLA Modules:
  0.0 87.9 jit_solution(3847625674256710787)
XLA Ops:
  0.6 0.0 copy-start
  0.6 1.9 %copy-done = bf16[1,256,6144]{2,1,0:T(8,128)(2,1)S(1)} copy-done((bf16[1,256,6144]{2,1,0:T(8,128)(2,1)S(1)}, bf16[1,256,6144]{2,1,0:T(8,128)(2,1)}, u32[]{:S(2)}) %copy-start) | copy-done | bytes 3145752
  2.5 0.0 copy-start.1
  2.5 1.0 %copy-done.1 = bf16[1,256,1024]{2,1,0:T(8,128)(2,1)S(1)} copy-done((bf16[1,256,1024]{2,1,0:T(8,128)(2,1)S(1)}, bf16[1,256,1024]{2,1,0:T(8,128)(2,1)}, u32[]{:S(2)}) %copy-start.1) | copy-done | bytes 524312
  3.6 0.0 copy-start.2
  3.6 0.9 %copy-done.2 = bf16[1,256,256]{2,1,0:T(8,128)(2,1)S(1)} copy-done((bf16[1,256,256]{2,1,0:T(8,128)(2,1)S(1)}, bf16[1,256,256]{2,1,0:T(8,128)(2,1)}, u32[]{:S(2)}) %copy-start.2) | copy-done | bytes 131096
  4.5 0.0 copy-start.3
  4.5 0.8 copy-done.3
  5.3 0.0 copy-start.4
  5.3 0.8 copy-done.4
  6.2 0.0 copy-start.5
  6.2 0.7 copy-done.5
  6.9 0.0 copy-start.6
  6.9 0.7 copy-done.6
  7.5 78.4 %shard_map.94 = (bf16[1,256,256]{2,1,0:T(8,128)(2,1)S(1)}, f32[1,256,128]{2,1,0:T(8,128)S(1)}, f32[128,256]{1,0:T(8,128)S(1)}) custom-call(bf16[1,256,128]{2,1,0:T(8,128)(2,1)S(1)} %copy-done.3, bf16[1,256,256]{2,1,0:T(8,128)(2,1)S(1)} %copy-done.2, bf16[128,256]{1,0:T(8,128)(2,1)S(1)} %copy-done.4, bf16[1,256,6144]{2,1,0:T(8,128)(2,1)S(1)} %copy-done, ...), custom_call_target="tpu_custom_call" | custom-call | tf_op jit(solution)/shard_map/pallas_call | solution.py:246
  85.9 0.7 copy.13
  86.6 0.7 copy.14
  87.2 0.7 copy.15
Async XLA Ops:
  0.6 1.9 %copy-start = (bf16[1,256,6144]{2,1,0:T(8,128)(2,1)S(1)}, bf16[1,256,6144]{2,1,0:T(8,128)(2,1)}, u32[]{:S(2)}) copy-start(bf16[1,256,6144]{2,1,0:T(8,128)(2,1)} %adj_hbm.1) | copy-start | bytes 9437188
  2.5 1.0 %copy-start.1 = (bf16[1,256,1024]{2,1,0:T(8,128)(2,1)S(1)}, bf16[1,256,1024]{2,1,0:T(8,128)(2,1)}, u32[]{:S(2)}) copy-start(bf16[1,256,1024]{2,1,0:T(8,128)(2,1)} %far_hbm.1) | copy-start | bytes 1572868
  3.6 0.9 %copy-start.2 = (bf16[1,256,256]{2,1,0:T(8,128)(2,1)S(1)}, bf16[1,256,256]{2,1,0:T(8,128)(2,1)}, u32[]{:S(2)}) copy-start(bf16[1,256,256]{2,1,0:T(8,128)(2,1)} %cotan.1) | copy-start | bytes 393220
  4.5 0.8 copy-start.3
  5.3 0.8 copy-start.4
  6.2 0.7 copy-start.5
  6.9 0.7 copy-start.6

commit v2 on v1

v2 whole, which is shorter than its diff:
```python
import functools
import math

import jax
import jax.numpy as jnp
from jax import lax
from jax.experimental import pallas as pl
from jax.experimental.pallas import tpu as pltpu
from jax.sharding import PartitionSpec as P

MESH = pl.DeviceIdType.MESH
F32 = jnp.float32
BF16 = jnp.bfloat16


def dot(a, b, dims=((1,), (0,))):
    return lax.dot_general(a, b, (dims, ((), ())), preferred_element_type=F32)

ROUTE = (
    (-1, 0, 1, 0, 16, 12),
    (-1, 2, 0, 0, 16, 4),
    (-1, -2, 0, 0, 16, 5),
    (-1, 1, 0, 0, 16, 13),
    (-1, -1, 0, 0, 16, 14),
    (1, 0, 1, 0, 16, 19),
    (2, 0, 1, 0, 16, 20),
    (1, 3, 0, 0, 16, 0),
    (2, -3, 0, 0, 16, 1),
    (3, 0, 1, 0, 16, 15),
    (1, 1, 0, 0, 16, 10),
    (2, -1, 0, 0, 16, 11),
    (4, 0, 1, 0, 16, 16),
    (5, 1, 0, 0, 16, 17),
    (6, -1, 0, 0, 16, 18),
    (7, 1, 0, 0, 8, 8),
    (8, -1, 0, 8, 16, 9),
    (7, 1, 1, 0, 8, 6),
    (7, 0, 1, 0, 16, 23),
    (10, 1, 0, 0, 16, 21),
    (11, -1, 0, 0, 16, 22),
    (8, -1, 1, 8, 16, 7),
    (13, 1, 0, 0, 16, 2),
    (8, 0, 1, 0, 16, 24),
    (14, -1, 0, 0, 16, 3),
)
GRAD_AT = (8, 18, 21)


def route_places():
    places = []
    for parent, dz, other, *_ in ROUTE:
        at = (0, 0) if parent < 0 else places[parent]
        places.append((at[0] - dz, at[1] ^ other))
    return places


def passed_on(parent):
    return sorted((k for k, entry in enumerate(ROUTE) if entry[0] == parent), key=lambda k: ROUTE[k][5])


def far_first(count):
    return sorted(range(count), key=lambda step: -min(step, count - step))


def layer_kernel(
    n_blk, n_rep,
    feats_hbm, cotan_hbm, weight_hbm, adj_hbm, far_hbm, ids_hbm, counts_hbm,
    out_rows, grad_feats, grad_weight,
    feats, cotan, weight, ids, counts,
    adj, far, near_x, near_p, total, pick, sent, arrived, back, returned, part, sum_rep, sum_blk, whole,
    load_sem, ring_send, ring_recv, swap_send, swap_recv, grad_send, grad_recv,
):
    blk = lax.axis_index("blk")
    rep = lax.axis_index("rep")
    rows, width = feats.shape
    groups, slots = ids.shape
    slot_total = groups * slots
    n_z = n_blk // 2
    n_y = n_rep // 4
    z = blk // 2
    x_hi = lax.rem(blk, 2)
    unit = rows // 16
    piece = part.shape[1]
    places = route_places()
    hops = sorted({(dz, other) for _, dz, other, *_ in ROUTE})

    def block_at(dz, other):
        return lax.rem(z + dz + 2 * n_z, n_z) * 2 + (1 - x_hi if other else x_hi)

    def rep_at(dy, low, core):
        x_low, y, own = rep // (2 * n_y), lax.rem(rep // 2, n_y), lax.rem(rep, 2)
        return lax.rem(x_low + low, 2) * (2 * n_y) + lax.rem(y + dy, n_y) * 2 + lax.rem(own + core, 2)

    barrier = pltpu.get_barrier_semaphore()

    for hop in hops:
        pl.semaphore_signal(barrier, inc=1, device_id={"blk": block_at(*hop)}, device_id_type=MESH)

    def greet_rep(i, carry):
        pl.semaphore_signal(barrier, inc=1, device_id={"rep": lax.rem(rep + i, n_rep)}, device_id_type=MESH)
        return carry

    lax.fori_loop(1, n_rep, greet_rep, 0)

    loads = [
        pltpu.make_async_copy(src, dst, load_sem.at[i])
        for i, (src, dst) in enumerate((
            (feats_hbm.at[0], feats), (ids_hbm.at[0, 0], ids), (counts_hbm.at[0], counts),
            (adj_hbm.at[0], adj), (far_hbm.at[0], far), (cotan_hbm.at[0], cotan), (weight_hbm, weight),
        ))
    ]
    for load in loads:
        load.start()

    def copy_on(near, phase, k):
        parent, dz, other, low, high, _ = ROUTE[k]
        at = block_at(*(places[parent] if parent >= 0 else (0, 0)))
        span = near.at[at, pl.ds(low * unit, (high - low) * unit)]
        return pltpu.make_async_remote_copy(
            src_ref=span, dst_ref=span, send_sem=ring_send.at[phase], recv_sem=ring_recv.at[phase, k],
            device_id={"blk": block_at(dz, other)}, device_id_type=MESH,
        )

    def wait_copy(near, phase, k):
        low, high = ROUTE[k][3:5]
        span = near.at[block_at(*places[k]), pl.ds(low * unit, (high - low) * unit)]
        pltpu.make_async_copy(span, span, ring_recv.at[phase, k]).wait()

    def add_block(near, idx):
        columns = pl.ds(pl.multiple_of(idx * rows, rows), rows)
        total[...] += dot(adj[:, columns], near[idx])

    def ring_open(near, phase):
        for k in passed_on(-1):
            copy_on(near, phase, k).start()

    def ring_run(near, phase, between):
        seen = {}
        for k in range(len(ROUTE)):
            wait_copy(near, phase, k)
            for child in passed_on(k):
                copy_on(near, phase, child).start()
            place = (places[k][0] % n_z, places[k][1])
            seen[place] = seen.get(place, 0) + ROUTE[k][4] - ROUTE[k][3]
            if seen[place] == 16:
                add_block(near, block_at(*place))
            for task in between.get(k, ()):
                task()

    def ring_drain(near, phase):
        whole_ring = near.at[pl.ds(0, n_blk - 1)]
        pltpu.make_async_copy(whole_ring, whole_ring, ring_send.at[phase]).wait()

    def to_reps(src, dst, send_sem, recv_sem, steps):
        for dy in steps:
            def send(i, carry, dy=dy):
                peer = rep_at(dy, i // 2, lax.rem(i, 2))
                pltpu.make_async_remote_copy(
                    src_ref=src(peer), dst_ref=dst, send_sem=send_sem, recv_sem=recv_sem,
                    device_id={"rep": peer}, device_id_type=MESH,
                ).start()
                return carry
            lax.fori_loop(0 if dy else 1, 4, send, 0)

    def wait_all(ref, count, sem):
        span = ref.at[pl.ds(0, count)]
        pltpu.make_async_copy(span, span, sem).wait()

    far_y = far_first(n_y)
    loads[0].wait()
    own_feats = feats[...]
    near_x[blk] = own_feats
    pl.semaphore_wait(barrier, n_rep - 1 + len(hops))
    ring_open(near_x, 0)

    spread = lax.broadcasted_iota(jnp.int32, (slots, slot_total), 1)
    within = spread - (spread // slots) * slots
    place = lax.broadcasted_iota(jnp.int32, (slots, slot_total), 0)
    per_slot = jnp.where(within == place, 1.0, 0.0).astype(BF16)
    spread_g = lax.broadcasted_iota(jnp.int32, (groups, slot_total), 1)
    own_group = (spread_g // slots) == lax.broadcasted_iota(jnp.int32, (groups, slot_total), 0)
    per_group = jnp.where(own_group, 1.0, 0.0).astype(BF16)
    loads[1].wait()
    ids_wide = dot(ids[...].astype(F32).astype(BF16), per_slot)
    ids_row = jnp.sum(jnp.where(own_group, ids_wide, 0.0), axis=0, keepdims=True)
    loads[2].wait()
    counts_low = jnp.broadcast_to(counts[...].astype(F32), (8, groups)).astype(BF16)
    counts_row = dot(counts_low, per_group)[0:1]
    live = within[0:1].astype(F32) < counts_row
    ids_row = jnp.where(live, ids_row, -1.0).astype(jnp.int32)
    row_iota = lax.broadcasted_iota(jnp.int32, (rows, slot_total), 0)
    pick[...] = jnp.where(row_iota == ids_row, 1.0, 0.0).astype(BF16)
    sent[...] = dot(pick[...], own_feats, ((0,), (0,))).astype(BF16).reshape(groups, slots, width)
    to_reps(lambda peer: sent.at[peer], arrived.at[rep], swap_send.at[0], swap_recv.at[0], far_y)
    arrived[rep] = sent[rep]

    total[...] = jnp.zeros_like(total)
    loads[3].wait()
    add_block(near_x, blk)

    def add_far():
        loads[4].wait()
        wait_all(arrived, n_rep - 1, swap_recv.at[0])
        total[...] += dot(far[...], arrived[...].reshape(slot_total, width))

    ring_run(near_x, 0, {len(ROUTE) - 5: (add_far,)})

    agg = total[...].astype(BF16)
    loads[5].wait()
    loads[6].wait()
    pre = dot(agg, weight[...])
    scale, cubic = 0.7978845608028654, 0.044715
    square = pre * pre
    bend = jnp.tanh(scale * pre * (1.0 + cubic * square))
    slope = 0.5 * (1.0 + bend) + 0.5 * pre * (1.0 - bend * bend) * (scale * (1.0 + 3.0 * cubic * square))
    dpre = (cotan[...].astype(F32) * slope).astype(BF16)
    proj = dot(dpre, weight[...], ((1,), (1,))).astype(BF16)
    near_p[blk] = proj
    ring_open(near_p, 1)
    share = dot(agg, dpre, ((0,), (0,)))
    per_half = n_rep // 2
    part[pl.ds(0, per_half)] = share[:, :width].reshape(per_half, piece, width)
    part[pl.ds(per_half, per_half)] = share[:, width:].reshape(per_half, piece, width)
    to_reps(lambda peer: part.at[peer], sum_rep.at[rep], grad_send.at[0], grad_recv.at[0], far_y)
    sum_rep[rep] = part[rep]
    out_rows[0] = (0.5 * pre * (1.0 + bend)).astype(BF16)
    back[...] = dot(far[...], proj, ((0,), (0,))).astype(BF16).reshape(groups, slots, width)
    returned[rep] = back[rep]
    total[...] = jnp.zeros_like(total)
    add_block(near_p, blk)

    def swap_back(steps):
        return lambda: to_reps(lambda peer: back.at[peer], returned.at[rep], swap_send.at[1], swap_recv.at[1], steps)

    def grad_blk():
        wait_all(sum_rep, n_rep - 1, grad_recv.at[0])
        sum_blk[blk] = jnp.sum(sum_rep[...], axis=0)
        for dz in far_first(n_z):
            for other in (1, 0):
                if dz or other:
                    pltpu.make_async_remote_copy(
                        src_ref=sum_blk.at[blk], dst_ref=sum_blk.at[blk],
                        send_sem=grad_send.at[1], recv_sem=grad_recv.at[1],
                        device_id={"blk": block_at(dz, other)}, device_id_type=MESH,
                    ).start()

    def grad_whole():
        wait_all(sum_blk, n_blk - 1, grad_recv.at[1])
        nodes = rows * n_blk * n_rep
        whole[rep] = jnp.sum(sum_blk[...], axis=0) * (1.0 / math.sqrt(nodes))
        to_reps(lambda peer: whole.at[rep], whole.at[rep], grad_send.at[2], grad_recv.at[2], far_y)

    def add_returned():
        wait_all(returned, n_rep - 1, swap_recv.at[1])
        total[...] += dot(pick[...], returned[...].reshape(slot_total, width))

    quarter = max(1, n_y // 4)
    tasks = {0: [swap_back(far_y[:quarter])], 2: [swap_back(far_y[quarter:2 * quarter])],
             4: [swap_back(far_y[2 * quarter:3 * quarter])], 5: [swap_back(far_y[3 * quarter:])]}
    for at, task in ((GRAD_AT[0], grad_blk), (GRAD_AT[1], grad_whole), (GRAD_AT[2], add_returned)):
        tasks.setdefault(at, []).append(task)
    ring_run(near_p, 1, tasks)

    grad_feats[0] = total[...]
    wait_all(whole, n_rep - 1, grad_recv.at[2])
    flat = per_half * piece
    grad_weight[:, :width] = whole[pl.ds(0, per_half)].reshape(flat, width)
    grad_weight[:, width:] = whole[pl.ds(per_half, per_half)].reshape(flat, width)

    ring_drain(near_x, 0)
    ring_drain(near_p, 1)
    wait_all(sent, n_rep - 1, swap_send.at[0])
    wait_all(back, n_rep - 1, swap_send.at[1])
    wait_all(part, n_rep - 1, grad_send.at[0])
    wait_all(sum_blk, n_blk - 1, grad_send.at[1])
    wait_all(whole, n_rep - 1, grad_send.at[2])


def hand_out(rows_in, feats_in, weight_in, rows_out, feats_out, weight_out, rows, feats, weight, sem):
    stages = ((rows_in, rows, rows_out), (feats_in, feats, feats_out), (weight_in, weight, weight_out))
    fetches = [pltpu.make_async_copy(src, held, sem.at[0, i]) for i, (src, held, _) in enumerate(stages)]
    stores = [pltpu.make_async_copy(held, dst, sem.at[1, i]) for i, (_, held, dst) in enumerate(stages)]
    for fetch in fetches:
        fetch.start()
    for fetch, store in zip(fetches, stores):
        fetch.wait()
        store.start()
    for store in stores:
        store.wait()


def local(n_blk, n_rep, feats, cotan, weight, cycle_adj, remote_adj, send_ids, send_count):
    rows, width = feats.shape[1:]
    hidden = cotan.shape[2]
    groups, slots = send_ids.shape[2:]
    total = n_blk * rows
    piece = hidden // n_rep * (width // 128)
    vmem = pl.BlockSpec(memory_space=pltpu.VMEM)
    anywhere = pl.BlockSpec(memory_space=pl.ANY)
    dma = pltpu.SemaphoreType.DMA
    results = pl.pallas_call(
        functools.partial(layer_kernel, n_blk, n_rep),
        out_shape=(
            jax.ShapeDtypeStruct((1, rows, hidden), BF16),
            jax.ShapeDtypeStruct((1, rows, width), F32),
            jax.ShapeDtypeStruct((width, hidden), F32),
        ),
        in_specs=[anywhere] * 7,
        out_specs=(vmem, vmem, vmem),
        scratch_shapes=[
            pltpu.VMEM((rows, width), BF16),
            pltpu.VMEM((rows, hidden), BF16),
            pltpu.VMEM((width, hidden), BF16),
            pltpu.VMEM((groups, slots), jnp.int32),
            pltpu.VMEM((1, groups), jnp.int32),
            pltpu.VMEM((rows, total), BF16),
            pltpu.VMEM((rows, groups * slots), BF16),
            pltpu.VMEM((n_blk, rows, width), BF16),
            pltpu.VMEM((n_blk, rows, width), BF16),
            pltpu.VMEM((rows, width), F32),
            pltpu.VMEM((rows, groups * slots), BF16),
            pltpu.VMEM((groups, slots, width), BF16),
            pltpu.VMEM((groups, slots, width), BF16),
            pltpu.VMEM((groups, slots, width), BF16),
            pltpu.VMEM((groups, slots, width), BF16),
            pltpu.VMEM((n_rep, piece, width), F32),
            pltpu.VMEM((n_rep, piece, width), F32),
            pltpu.VMEM((n_blk, piece, width), F32),
            pltpu.VMEM((n_rep, piece, width), F32),
            dma((7,)),
            dma((2,)),
            dma((2, len(ROUTE))),
            dma((2,)),
            dma((2,)),
            dma((3,)),
            dma((3,)),
        ],
        compiler_params=pltpu.CompilerParams(
            collective_id=0, has_side_effects=True, vmem_limit_bytes=60 * 1024 * 1024
        ),
    )(feats, cotan, weight, cycle_adj, remote_adj, send_ids, send_count)
    return pl.pallas_call(
        hand_out,
        out_shape=tuple(jax.ShapeDtypeStruct(value.shape, value.dtype) for value in results),
        in_specs=[anywhere] * 3,
        out_specs=(anywhere,) * 3,
        scratch_shapes=[pltpu.VMEM(value.shape, value.dtype) for value in results] + [dma((2, 3))],
        compiler_params=pltpu.CompilerParams(vmem_limit_bytes=60 * 1024 * 1024),
    )(*results)


def solution(mesh):
    n_blk, n_rep = mesh.shape["blk"], mesh.shape["rep"]
    return jax.shard_map(
        functools.partial(local, n_blk, n_rep),
        mesh=mesh,
        in_specs=(
            P("rep", "blk", None),
            P("rep", "blk", None),
            P(),
            P("rep", "blk", None),
            P("rep", "blk", None),
            P("rep", "blk", None, None),
            P("rep", "blk", None),
        ),
        out_specs=(P("rep", "blk", None), P("rep", "blk", None), P()),
        check_vma=False,
    )
```

time: 88.3 us -> 71.1 us (0.81)
  local copies, waits for them, and re-layouts: 8.84 us -> 0 us
  Pallas kernels: 78.4 us -> 70.3 us
    pallas_call x1, Pallas kernels: 78.4 us -> 68.5 us  [local(): pl.pallas_call(functools.partial(layer_kernel, n_blk, n_rep), out_shape=(...]
    unnamed x17 -> x0, local copies, waits for them, and re-layouts: 8.84 us -> none
    pallas_call x0 -> x1, Pallas kernels: none -> 1.74 us  [local(): pl.pallas_call(hand_out, out_shape=tuple((jax.ShapeDtypeStruct(value.shap...]
where the time goes in v2:
time: 71.1 us; the launch traced here: 70.9 us
  Pallas kernels  70.3 us (99%)
    pallas_call x1, Pallas kernels, local(): pl.pallas_call(functools.partial(layer_kernel, n_blk, n_rep), out_shape=(...  68.5 us
    pallas_call x1, Pallas kernels, local(): pl.pallas_call(hand_out, out_shape=tuple((jax.ShapeDtypeStruct(value.shap...  1.74 us

profile of v2, /device:TPU:1, one launch (start us, length us, event | category | flops | bytes accessed | tf_op | source)
XLA Modules:
  0.0 70.9 jit_solution(13276115038197978956)
XLA Ops:
  0.6 68.5 %shard_map.94 = (bf16[1,256,256]{2,1,0:T(8,128)(2,1)}, f32[1,256,128]{2,1,0:T(8,128)}, f32[128,256]{1,0:T(8,128)}) custom-call(bf16[1,256,128]{2,1,0:T(8,128)(2,1)} %feats_hbm.1, bf16[1,256,256]{2,1,0:T(8,128)(2,1)} %cotan_hbm.1, bf16[128,256]{1,0:T(8,128)(2,1)} %weight_hbm.1, bf16[1,256,6144]{2,1,0:T(8,128)(2,1)} %adj_hbm.1, bf16[1,256,1024]{2,1,0:T(8,128)(2,1)} %far_hbm.1, ...), custom_call_target="tpu_custom_call" | custom-call | tf_op jit(solution)/shard_map/pallas_call | solution.py:301
  69.2 1.7 %shard_map.95 = (bf16[1,256,256]{2,1,0:T(8,128)(2,1)}, f32[1,256,128]{2,1,0:T(8,128)}, f32[128,256]{1,0:T(8,128)}) custom-call(bf16[1,256,256]{2,1,0:T(8,128)(2,1)} %get-tuple-element.6.rows_in, f32[1,256,128]{2,1,0:T(8,128)} %get-tuple-element.7.feats_in, f32[128,256]{1,0:T(8,128)} %get-tuple-element.8.weight_in), custom_call_target="tpu_custom_call" | custom-call | tf_op jit(solution)/shard_map/pallas_call | solution.py:342

commit v3 on v2

--- a/solution.py
+++ b/solution.py
@@ -17,33 +17,59 @@
     return lax.dot_general(a, b, (dims, ((), ())), preferred_element_type=F32)
 
 ROUTE = (
-    (-1, 0, 1, 0, 16, 12),
-    (-1, 2, 0, 0, 16, 4),
-    (-1, -2, 0, 0, 16, 5),
-    (-1, 1, 0, 0, 16, 13),
-    (-1, -1, 0, 0, 16, 14),
-    (1, 0, 1, 0, 16, 19),
-    (2, 0, 1, 0, 16, 20),
-    (1, 3, 0, 0, 16, 0),
-    (2, -3, 0, 0, 16, 1),
-    (3, 0, 1, 0, 16, 15),
-    (1, 1, 0, 0, 16, 10),
-    (2, -1, 0, 0, 16, 11),
-    (4, 0, 1, 0, 16, 16),
-    (5, 1, 0, 0, 16, 17),
-    (6, -1, 0, 0, 16, 18),
-    (7, 1, 0, 0, 8, 8),
-    (8, -1, 0, 8, 16, 9),
-    (7, 1, 1, 0, 8, 6),
-    (7, 0, 1, 0, 16, 23),
-    (10, 1, 0, 0, 16, 21),
-    (11, -1, 0, 0, 16, 22),
-    (8, -1, 1, 8, 16, 7),
-    (13, 1, 0, 0, 16, 2),
-    (8, 0, 1, 0, 16, 24),
-    (14, -1, 0, 0, 16, 3),
+    (-1, 1, 0, 0, 8, 4),
+    (-1, -1, 0, 0, 8, 5),
+    (-1, 0, 1, 8, 16, 30),
+    (-1, 0, 1, 0, 8, 35),
+    (-1, 2, 0, 8, 16, 40),
+    (-1, -2, 0, 8, 16, 41),
+    (-1, 1, 0, 8, 16, 48),
+    (-1, -1, 0, 8, 16, 49),
+    (0, 0, 1, 0, 8, 22),
+    (0, 2, 0, 0, 8, 10),
+    (0, 1, 0, 0, 8, 20),
+    (1, -2, 0, 0, 8, 11),
+    (1, 0, 1, 0, 8, 23),
+    (1, -1, 0, 0, 8, 21),
+    (4, 1, 0, 8, 16, 18),
+    (4, 0, 1, 8, 16, 2),
+    (5, -1, 0, 8, 16, 19),
+    (5, 0, 1, 8, 16, 3),
+    (6, 0, 1, 8, 16, 8),
+    (9, 1, 0, 0, 8, 14),
+    (7, 0, 1, 8, 16, 9),
+    (11, -1, 0, 0, 8, 15),
+    (4, 4, 0, 8, 12, 36),
+    (9, 0, 1, 0, 8, 31),
+    (5, -4, 0, 12, 16, 37),
+    (14, 1, 0, 8, 16, 33),
+    (10, 0, 1, 0, 8, 16),
+    (9, 3, 0, 0, 4, 42),
+    (16, -1, 0, 8, 16, 34),
+    (11, 0, 1, 0, 8, 32),
+    (11, -3, 0, 4, 8, 43),
+    (13, 0, 1, 0, 8, 17),
+    (15, 2, 0, 8, 16, 26),
+    (19, 1, 0, 0, 8, 0),
+    (14, 0, 1, 8, 16, 24),
+    (17, -2, 0, 8, 16, 27),
+    (21, -1, 0, 0, 8, 1),
+    (16, 0, 1, 8, 16, 25),
+    (23, 1, 0, 0, 8, 12),
+    (28, -1, 0, 8, 16, 39),
+    (25, 1, 0, 8, 16, 38),
+    (19, 1, 1, 0, 8, 6),
+    (22, 0, 1, 8, 12, 44),
+    (29, -1, 0, 0, 8, 13),
+    (32, 1, 0, 8, 16, 28),
+    (21, -1, 1, 0, 8, 7),
+    (24, 0, 1, 12, 16, 45),
+    (27, 0, 1, 0, 4, 46),
+    (35, -1, 0, 8, 16, 29),
+    (30, 0, 1, 4, 8, 47),
 )
-GRAD_AT = (8, 18, 21)
+GRAD_AT = (10, 26, 46)
+BACK_AT = (11, 13, 15, 17)
 
 
 def route_places():
@@ -87,20 +113,23 @@
     def block_at(dz, other):
         return lax.rem(z + dz + 2 * n_z, n_z) * 2 + (1 - x_hi if other else x_hi)
 
-    def rep_at(dy, low, core):
-        x_low, y, own = rep // (2 * n_y), lax.rem(rep // 2, n_y), lax.rem(rep, 2)
-        return lax.rem(x_low + low, 2) * (2 * n_y) + lax.rem(y + dy, n_y) * 2 + lax.rem(own + core, 2)
+    x_low, y, core = rep // (2 * n_y), lax.rem(rep // 2, n_y), lax.rem(rep, 2)
+    x_parts = (x_low * (2 * n_y), (1 - x_low) * (2 * n_y))
+    y_parts = [lax.rem(y + dy, n_y) * 2 for dy in range(n_y)]
+    core_parts = (core, 1 - core)
+    steps = [(dy, dx, dc) for dy in range(n_y) for dx in (0, 1) for dc in (0, 1) if dy or dx or dc]
+    steps.sort(key=lambda step: -min(step[0], n_y - step[0]) - step[1])
+    peers = [x_parts[dx] + y_parts[dy] + core_parts[dc] for dy, dx, dc in steps]
+    fourth = n_rep // 4
+    fourths = [peers[i:i + fourth] for i in range(0, n_rep - 1, fourth)]
 
     barrier = pltpu.get_barrier_semaphore()
 
     for hop in hops:
         pl.semaphore_signal(barrier, inc=1, device_id={"blk": block_at(*hop)}, device_id_type=MESH)
 
-    def greet_rep(i, carry):
-        pl.semaphore_signal(barrier, inc=1, device_id={"rep": lax.rem(rep + i, n_rep)}, device_id_type=MESH)
-        return carry
-
-    lax.fori_loop(1, n_rep, greet_rep, 0)
+    for peer in peers:
+        pl.semaphore_signal(barrier, inc=1, device_id={"rep": peer}, device_id_type=MESH)
 
     loads = [
         pltpu.make_async_copy(src, dst, load_sem.at[i])
@@ -126,24 +155,27 @@
         span = near.at[block_at(*places[k]), pl.ds(low * unit, (high - low) * unit)]
         pltpu.make_async_copy(span, span, ring_recv.at[phase, k]).wait()
 
-    def add_block(near, idx):
-        columns = pl.ds(pl.multiple_of(idx * rows, rows), rows)
-        total[...] += dot(adj[:, columns], near[idx])
+    def add_pair(near, dz):
+        first = lax.rem(z + dz + n_z, n_z) * 2
+        columns = pl.ds(pl.multiple_of(first * rows, 2 * rows), 2 * rows)
+        total[...] += dot(adj[:, columns], near[pl.ds(first, 2)].reshape(2 * rows, width))
 
     def ring_open(near, phase):
         for k in passed_on(-1):
             copy_on(near, phase, k).start()
 
     def ring_run(near, phase, between):
-        seen = {}
+        seen = {0: 16}
+        for task in between.get(-1, ()):
+            task()
         for k in range(len(ROUTE)):
             wait_copy(near, phase, k)
             for child in passed_on(k):
                 copy_on(near, phase, child).start()
-            place = (places[k][0] % n_z, places[k][1])
+            place = places[k][0] % n_z
             seen[place] = seen.get(place, 0) + ROUTE[k][4] - ROUTE[k][3]
-            if seen[place] == 16:
-                add_block(near, block_at(*place))
+            if seen[place] == 32:
+                add_pair(near, place)
             for task in between.get(k, ()):
                 task()
 
@@ -151,59 +183,59 @@
         whole_ring = near.at[pl.ds(0, n_blk - 1)]
         pltpu.make_async_copy(whole_ring, whole_ring, ring_send.at[phase]).wait()
 
-    def to_reps(src, dst, send_sem, recv_sem, steps):
-        for dy in steps:
-            def send(i, carry, dy=dy):
-                peer = rep_at(dy, i // 2, lax.rem(i, 2))
-                pltpu.make_async_remote_copy(
-                    src_ref=src(peer), dst_ref=dst, send_sem=send_sem, recv_sem=recv_sem,
-                    device_id={"rep": peer}, device_id_type=MESH,
-                ).start()
-                return carry
-            lax.fori_loop(0 if dy else 1, 4, send, 0)
+    def to_reps(src, dst, send_sem, recv_sem, chosen):
+        for peer in chosen:
+            pltpu.make_async_remote_copy(
+                src_ref=src(peer), dst_ref=dst, send_sem=send_sem, recv_sem=recv_sem,
+                device_id={"rep": peer}, device_id_type=MESH,
+            ).start()
 
     def wait_all(ref, count, sem):
         span = ref.at[pl.ds(0, count)]
         pltpu.make_async_copy(span, span, sem).wait()
 
-    far_y = far_first(n_y)
     loads[0].wait()
     own_feats = feats[...]
     near_x[blk] = own_feats
     pl.semaphore_wait(barrier, n_rep - 1 + len(hops))
     ring_open(near_x, 0)
 
-    spread = lax.broadcasted_iota(jnp.int32, (slots, slot_total), 1)
-    within = spread - (spread // slots) * slots
-    place = lax.broadcasted_iota(jnp.int32, (slots, slot_total), 0)
-    per_slot = jnp.where(within == place, 1.0, 0.0).astype(BF16)
-    spread_g = lax.broadcasted_iota(jnp.int32, (groups, slot_total), 1)
-    own_group = (spread_g // slots) == lax.broadcasted_iota(jnp.int32, (groups, slot_total), 0)
-    per_group = jnp.where(own_group, 1.0, 0.0).astype(BF16)
-    loads[1].wait()
-    ids_wide = dot(ids[...].astype(F32).astype(BF16), per_slot)
-    ids_row = jnp.sum(jnp.where(own_group, ids_wide, 0.0), axis=0, keepdims=True)
-    loads[2].wait()
-    counts_low = jnp.broadcast_to(counts[...].astype(F32), (8, groups)).astype(BF16)
-    counts_row = dot(counts_low, per_group)[0:1]
-    live = within[0:1].astype(F32) < counts_row
-    ids_row = jnp.where(live, ids_row, -1.0).astype(jnp.int32)
-    row_iota = lax.broadcasted_iota(jnp.int32, (rows, slot_total), 0)
-    pick[...] = jnp.where(row_iota == ids_row, 1.0, 0.0).astype(BF16)
-    sent[...] = dot(pick[...], own_feats, ((0,), (0,))).astype(BF16).reshape(groups, slots, width)
-    to_reps(lambda peer: sent.at[peer], arrived.at[rep], swap_send.at[0], swap_recv.at[0], far_y)
-    arrived[rep] = sent[rep]
-
-    total[...] = jnp.zeros_like(total)
-    loads[3].wait()
-    add_block(near_x, blk)
+    def make_pick():
+        spread = lax.broadcasted_iota(jnp.int32, (slots, slot_total), 1)
+        within = spread - (spread // slots) * slots
+        place = lax.broadcasted_iota(jnp.int32, (slots, slot_total), 0)
+        per_slot = jnp.where(within == place, 1.0, 0.0).astype(BF16)
+        spread_g = lax.broadcasted_iota(jnp.int32, (groups, slot_total), 1)
+        own_group = (spread_g // slots) == lax.broadcasted_iota(jnp.int32, (groups, slot_total), 0)
+        per_group = jnp.where(own_group, 1.0, 0.0).astype(BF16)
+        loads[1].wait()
+        ids_wide = dot(ids[...].astype(F32).astype(BF16), per_slot)
+        ids_row = jnp.sum(jnp.where(own_group, ids_wide, 0.0), axis=0, keepdims=True)
+        loads[2].wait()
+        counts_low = jnp.broadcast_to(counts[...].astype(F32), (8, groups)).astype(BF16)
+        counts_row = dot(counts_low, per_group)[0:1]
+        live = within[0:1].astype(F32) < counts_row
+        ids_row = jnp.where(live, ids_row, -1.0).astype(jnp.int32)
+        row_iota = lax.broadcasted_iota(jnp.int32, (rows, slot_total), 0)
+        pick[...] = jnp.where(row_iota == ids_row, 1.0, 0.0).astype(BF16)
+
+    def gather_slots():
+        sent[...] = dot(pick[...], feats[...], ((0,), (0,))).astype(BF16).reshape(groups, slots, width)
+        arrived[rep] = sent[rep]
+
+    def swap_out(chosen):
+        return lambda: to_reps(lambda peer: sent.at[peer], arrived.at[rep], swap_send.at[0], swap_recv.at[0], chosen)
+
+    def ready_adj():
+        total[...] = jnp.zeros_like(total)
+        loads[3].wait()
 
     def add_far():
         loads[4].wait()
         wait_all(arrived, n_rep - 1, swap_recv.at[0])
         total[...] += dot(far[...], arrived[...].reshape(slot_total, width))
 
-    ring_run(near_x, 0, {len(ROUTE) - 5: (add_far,)})
+    ring_run(near_x, 0, {-1: [make_pick, gather_slots, swap_out(peers), ready_adj], len(ROUTE) - 8: [add_far]})
 
     agg = total[...].astype(BF16)
     loads[5].wait()
@@ -221,16 +253,17 @@
     per_half = n_rep // 2
     part[pl.ds(0, per_half)] = share[:, :width].reshape(per_half, piece, width)
     part[pl.ds(per_half, per_half)] = share[:, width:].reshape(per_half, piece, width)
-    to_reps(lambda peer: part.at[peer], sum_rep.at[rep], grad_send.at[0], grad_recv.at[0], far_y)
+    to_reps(lambda peer: part.at[peer], sum_rep.at[rep], grad_send.at[0], grad_recv.at[0], peers)
     sum_rep[rep] = part[rep]
+    total[...] = jnp.zeros_like(total)
     out_rows[0] = (0.5 * pre * (1.0 + bend)).astype(BF16)
-    back[...] = dot(far[...], proj, ((0,), (0,))).astype(BF16).reshape(groups, slots, width)
-    returned[rep] = back[rep]
-    total[...] = jnp.zeros_like(total)
-    add_block(near_p, blk)
-
-    def swap_back(steps):
-        return lambda: to_reps(lambda peer: back.at[peer], returned.at[rep], swap_send.at[1], swap_recv.at[1], steps)
+
+    def make_back():
+        back[...] = dot(far[...], near_p[blk], ((0,), (0,))).astype(BF16).reshape(groups, slots, width)
+        returned[rep] = back[rep]
+
+    def swap_back(chosen):
+        return lambda: to_reps(lambda peer: back.at[peer], returned.at[rep], swap_send.at[1], swap_recv.at[1], chosen)
 
     def grad_blk():
         wait_all(sum_rep, n_rep - 1, grad_recv.at[0])
@@ -248,15 +281,15 @@
         wait_all(sum_blk, n_blk - 1, grad_recv.at[1])
         nodes = rows * n_blk * n_rep
         whole[rep] = jnp.sum(sum_blk[...], axis=0) * (1.0 / math.sqrt(nodes))
-        to_reps(lambda peer: whole.at[rep], whole.at[rep], grad_send.at[2], grad_recv.at[2], far_y)
+        to_reps(lambda peer: whole.at[rep], whole.at[rep], grad_send.at[2], grad_recv.at[2], peers)
 
     def add_returned():
         wait_all(returned, n_rep - 1, swap_recv.at[1])
         total[...] += dot(pick[...], returned[...].reshape(slot_total, width))
 
-    quarter = max(1, n_y // 4)
-    tasks = {0: [swap_back(far_y[:quarter])], 2: [swap_back(far_y[quarter:2 * quarter])],
-             4: [swap_back(far_y[2 * quarter:3 * quarter])], 5: [swap_back(far_y[3 * quarter:])]}
+    tasks = {8: [make_back]}
+    for at, chosen in zip(BACK_AT, fourths):
+        tasks.setdefault(at, []).append(swap_back(chosen))
     for at, task in ((GRAD_AT[0], grad_blk), (GRAD_AT[1], grad_whole), (GRAD_AT[2], add_returned)):
         tasks.setdefault(at, []).append(task)
     ring_run(near_p, 1, tasks)

time: 71.1 us -> 67.2 us (0.945)
  Pallas kernels: 70.3 us -> 66.4 us
    pallas_call x1, Pallas kernels: 68.5 us -> 64.7 us  [local(): pl.pallas_call(functools.partial(layer_kernel, n_blk, n_rep), out_shape=(...]
where the time goes in v3:
time: 67.2 us; the launch traced here: 67 us
  Pallas kernels  66.4 us (99%)
    pallas_call x1, Pallas kernels, local(): pl.pallas_call(functools.partial(layer_kernel, n_blk, n_rep), out_shape=(...  64.7 us
    pallas_call x1, Pallas kernels, local(): pl.pallas_call(hand_out, out_shape=tuple((jax.ShapeDtypeStruct(value.shap...  1.74 us

profile of v3, /device:TPU:1, one launch (start us, length us, event | category | flops | bytes accessed | tf_op | source)
XLA Modules:
  0.0 67.0 jit_solution(10658590120383350852)
XLA Ops:
  0.6 64.7 %shard_map.94 = (bf16[1,256,256]{2,1,0:T(8,128)(2,1)}, f32[1,256,128]{2,1,0:T(8,128)}, f32[128,256]{1,0:T(8,128)}) custom-call(bf16[1,256,128]{2,1,0:T(8,128)(2,1)} %feats_hbm.1, bf16[1,256,256]{2,1,0:T(8,128)(2,1)} %cotan_hbm.1, bf16[128,256]{1,0:T(8,128)(2,1)} %weight_hbm.1, bf16[1,256,6144]{2,1,0:T(8,128)(2,1)} %adj_hbm.1, bf16[1,256,1024]{2,1,0:T(8,128)(2,1)} %far_hbm.1, ...), custom_call_target="tpu_custom_call" | custom-call | tf_op jit(solution)/shard_map/pallas_call | solution.py:334
  65.3 1.7 %shard_map.95 = (bf16[1,256,256]{2,1,0:T(8,128)(2,1)}, f32[1,256,128]{2,1,0:T(8,128)}, f32[128,256]{1,0:T(8,128)}) custom-call(bf16[1,256,256]{2,1,0:T(8,128)(2,1)} %get-tuple-element.6.rows_in, f32[1,256,128]{2,1,0:T(8,128)} %get-tuple-element.7.feats_in, f32[128,256]{1,0:T(8,128)} %get-tuple-element.8.weight_in), custom_call_target="tpu_custom_call" | custom-call | tf_op jit(solution)/shard_map/pallas_call | solution.py:375

commit v4 on v3

--- a/solution.py
+++ b/solution.py
@@ -68,8 +68,8 @@
     (35, -1, 0, 8, 16, 29),
     (30, 0, 1, 4, 8, 47),
 )
-GRAD_AT = (10, 26, 46)
-BACK_AT = (11, 13, 15, 17)
+GRAD_AT = (8, 24, 46)
+BACK_AT = (-1, -1, -1, -1)
 
 
 def route_places():
@@ -256,7 +256,6 @@
     to_reps(lambda peer: part.at[peer], sum_rep.at[rep], grad_send.at[0], grad_recv.at[0], peers)
     sum_rep[rep] = part[rep]
     total[...] = jnp.zeros_like(total)
-    out_rows[0] = (0.5 * pre * (1.0 + bend)).astype(BF16)
 
     def make_back():
         back[...] = dot(far[...], near_p[blk], ((0,), (0,))).astype(BF16).reshape(groups, slots, width)
@@ -287,7 +286,11 @@
         wait_all(returned, n_rep - 1, swap_recv.at[1])
         total[...] += dot(pick[...], returned[...].reshape(slot_total, width))
 
-    tasks = {8: [make_back]}
+    tasks = {-1: [make_back]}
+    def put_rows():
+        out_rows[0] = (0.5 * pre * (1.0 + bend)).astype(BF16)
+
+    tasks[36] = [put_rows]
     for at, chosen in zip(BACK_AT, fourths):
         tasks.setdefault(at, []).append(swap_back(chosen))
     for at, task in ((GRAD_AT[0], grad_blk), (GRAD_AT[1], grad_whole), (GRAD_AT[2], add_returned)):

time: 67.2 us -> 65.6 us (0.976)
  Pallas kernels: 66.4 us -> 64.8 us
    pallas_call x1, Pallas kernels: 64.7 us -> 63.1 us  [local(): pl.pallas_call(functools.partial(layer_kernel, n_blk, n_rep), out_shape=(...]
where the time goes in v4:
time: 65.6 us; the launch traced here: 65.5 us
  Pallas kernels  64.8 us (99%)
    pallas_call x1, Pallas kernels, local(): pl.pallas_call(functools.partial(layer_kernel, n_blk, n_rep), out_shape=(...  63.1 us
    pallas_call x1, Pallas kernels, local(): pl.pallas_call(hand_out, out_shape=tuple((jax.ShapeDtypeStruct(value.shap...  1.74 us

profile of v4, /device:TPU:1, one launch (start us, length us, event | category | flops | bytes accessed | tf_op | source)
XLA Modules:
  0.0 65.5 jit_solution(14393312125706955036)
XLA Ops:
  0.6 63.1 %shard_map.94 = (bf16[1,256,256]{2,1,0:T(8,128)(2,1)}, f32[1,256,128]{2,1,0:T(8,128)}, f32[128,256]{1,0:T(8,128)}) custom-call(bf16[1,256,128]{2,1,0:T(8,128)(2,1)} %feats_hbm.1, bf16[1,256,256]{2,1,0:T(8,128)(2,1)} %cotan_hbm.1, bf16[128,256]{1,0:T(8,128)(2,1)} %weight_hbm.1, bf16[1,256,6144]{2,1,0:T(8,128)(2,1)} %adj_hbm.1, bf16[1,256,1024]{2,1,0:T(8,128)(2,1)} %far_hbm.1, ...), custom_call_target="tpu_custom_call" | custom-call | tf_op jit(solution)/shard_map/pallas_call | solution.py:337
  63.7 1.7 %shard_map.95 = (bf16[1,256,256]{2,1,0:T(8,128)(2,1)}, f32[1,256,128]{2,1,0:T(8,128)}, f32[128,256]{1,0:T(8,128)}) custom-call(bf16[1,256,256]{2,1,0:T(8,128)(2,1)} %get-tuple-element.6.rows_in, f32[1,256,128]{2,1,0:T(8,128)} %get-tuple-element.7.feats_in, f32[128,256]{1,0:T(8,128)} %get-tuple-element.8.weight_in), custom_call_target="tpu_custom_call" | custom-call | tf_op jit(solution)/shard_map/pallas_call | solution.py:378
